TPU v7x, 256 devices: a whole 4x4x8 slice. The times are simulated.
256 devices in a mesh: rep: 16 (over x, y_hi, core), shard: 16 (over z, y_lo).
Axes of the slice: x: 4, y: 4 (y_hi: 2, y_lo: 2; y = y_hi * 2 + y_lo), z: 8, core: 2. Of those that a mesh axis runs over, the one named last changes fastest.
Arguments:
- tokens: bfloat16 [65536, 5120], P(('rep', 'shard')), may hold values from -12 to 12
- key_weight: bfloat16 [5120, 1024], P('shard'), may hold values from -0.2 to 0.2
- key_gain: float32 [1024], replicated, may hold values from 0.1 to 1.9
- key_cotangent: bfloat16 [65536, 1024], P(('rep', 'shard')), may hold values from -6 to 6
Outputs:
- grad_tokens: bfloat16 [65536, 5120], P(('rep', 'shard'))
- grad_weight: float32 [5120, 1024], P('shard')
- grad_gain: float32 [1024], replicated
All inputs are finite; a program needn't handle non-finite values.
Results may differ from a plain program's by a relative error of at most 0.0049.
Values may be sent and summed in bfloat16 or wider, within the bound.
A program may use at most 128 MiB of HBM per device.

v0:
```python
import jax
import jax.numpy as jnp
from jax import lax
from jax.sharding import PartitionSpec as P

BUCKETS = 4


def per_device(tokens, key_weight, key_gain, key_cotangent):
    features = tokens.shape[1]
    key_width = key_weight.shape[1]
    n_shard = lax.axis_size("shard")
    devices = lax.axis_size("rep") * n_shard
    rows_here = features // n_shard
    gathered = lax.all_gather(key_weight, "shard", axis=0, tiled=True)
    projected = jnp.dot(tokens, gathered, preferred_element_type=jnp.float32)
    inverse = lax.rsqrt(jnp.mean(projected * projected, axis=1, keepdims=True) + 1e-06)
    normed = projected * inverse
    cotang = key_cotangent.astype(jnp.float32)
    scaled = cotang * key_gain
    dot_mean = jnp.mean(scaled * normed, axis=1, keepdims=True)
    grad_keys = (inverse * (scaled - normed * dot_mean)).astype(jnp.bfloat16)
    gain_part = jnp.sum(cotang * normed, axis=0)
    grad_tokens = lax.dot_general(
        grad_keys, gathered, (((1,), (1,)), ((), ())), preferred_element_type=jnp.float32
    ).astype(jnp.bfloat16)
    bucket_width = key_width // BUCKETS
    results = []
    for bucket in range(BUCKETS):
        bucket_grad = grad_keys[:, bucket * bucket_width : (bucket + 1) * bucket_width]

        def term(offset, count, bucket_grad=bucket_grad):
            return lax.dot_general(
                tokens, bucket_grad, (((0,), (0,)), ((), ())), preferred_element_type=jnp.float32
            )

        owned = lax.psum_scatter(
            term(jnp.int32(0), lax.axis_size("shard") * rows_here),
            "shard",
            scatter_dimension=0,
            tiled=True,
        )
        owned = lax.psum(owned, "rep")
        results.append(owned)
    summed = jnp.concatenate(results, axis=1)
    grad_weight = summed / devices
    grad_gain = lax.psum(gain_part, ("rep", "shard")) / devices
    return (grad_tokens, grad_weight, grad_gain)


def solution(mesh):
    return jax.shard_map(
        per_device,
        mesh=mesh,
        in_specs=(P(("rep", "shard"), None), P("shard", None), P(), P(("rep", "shard"), None)),
        out_specs=(P(("rep", "shard"), None), P("shard", None), P()),
        check_vma=False,
    )
```

profile of v0, /device:TPU:1, one launch (start us, length us, event | category | flops | bytes accessed | tf_op | source)
XLA Modules:
  0.0 906.7 jit_solution(12278927073362692079)
XLA Ops:
  7.2 0.0 copy-start
  7.2 0.0 all-gather.2.cloned.1.call-start
  7.2 0.7 all-gather.2.cloned.1.call-update
  7.9 0.0 copy-start.1
  7.9 0.0 copy-start.3
  7.9 0.0 reduce-scatter.19.cloned.1.call-start
  8.0 230.2 %all-gather.2.cloned.1.call-done = bf16[5120,1024]{1,0:T(8,128)(2,1)} async-done(((bf16[320,1024]{1,0:T(8,128)(2,1)}), bf16[5120,1024]{1,0:T(8,128)(2,1)}) %all-gather.2.cloned.1.call-update) | async-done | bytes 10485776 | tf_op jit(solution)/shard_map/all_gather | solution.py:15
  238.2 0.0 copy-done
  238.2 0.0 copy-start.2
  238.2 5.8 multiply_reduce_fusion
  244.0 0.0 copy-done.1
  244.0 0.0 copy-done.3
  244.0 0.4 fusion.5
  244.5 0.0 copy-done.2
  244.5 0.3 fusion.4
  244.8 3.1 convolution_bitcast_fusion
  247.9 5.9 copy.15
  253.7 0.0 reduce-scatter.19.cloned.1.call-update
  253.8 0.0 reduce-scatter.17.cloned.1.call-start
  253.8 3.2 convolution_bitcast_fusion.1
  257.0 5.9 copy.13
  262.9 0.0 reduce-scatter.17.cloned.1.call-update
  262.9 0.0 reduce-scatter.15.cloned.1.call-start
  263.0 3.3 convolution_bitcast_fusion.2
  266.2 6.0 copy.11
  272.2 0.0 reduce-scatter.15.cloned.1.call-update
  272.2 0.0 reduce-scatter.13.cloned.1.call-start
  272.3 3.2 convolution_bitcast_fusion.3
  275.4 6.0 copy.9
  281.4 0.0 reduce-scatter.13.cloned.1.call-update
  281.4 0.0 all-reduce.3.cloned.1.call-start
  281.5 92.8 %reduce-scatter.19.cloned.1.call-done = f32[320,256]{1,0:T(8,128)} async-done(((f32[5120,256]{1,0:T(8,128)}), f32[320,256]{1,0:T(8,128)}) %reduce-scatter.19.cloned.1.call-update) | async-done | bytes 327696
  374.2 1.9 copy.16
  376.1 121.0 %reduce-scatter.17.cloned.1.call-done = f32[320,256]{1,0:T(8,128)} async-done(((f32[5120,256]{1,0:T(8,128)}), f32[320,256]{1,0:T(8,128)}) %reduce-scatter.17.cloned.1.call-update) | async-done | bytes 327696
  497.1 1.9 copy.14
  499.0 120.8 %reduce-scatter.15.cloned.1.call-done = f32[320,256]{1,0:T(8,128)} async-done(((f32[5120,256]{1,0:T(8,128)}), f32[320,256]{1,0:T(8,128)}) %reduce-scatter.15.cloned.1.call-update) | async-done | bytes 327696
  619.8 1.9 copy.12
  621.7 120.8 %reduce-scatter.13.cloned.1.call-done = f32[320,256]{1,0:T(8,128)} async-done(((f32[5120,256]{1,0:T(8,128)}), f32[320,256]{1,0:T(8,128)}) %reduce-scatter.13.cloned.1.call-update) | async-done | bytes 327696
  742.5 1.9 copy.10
  744.5 0.0 all-reduce.3.cloned.1.call-update
  744.5 79.2 %psum.39 = f32[1024]{0:T(1024)S(1)} all-reduce(f32[1024]{0:T(1024)S(1)} %get-tuple-element.9), channel_id=1, replica_groups=mesh['rep'=16,'shard'=16] {'rep','shard'}, use_global_device_ids=true, to_apply=%region_11.0 | all-reduce | flops 1024 | bytes 8192 | tf_op jit(solution)/shard_map/psum | solution.py:47
  823.7 0.6 broadcast_multiply_fusion
  824.3 12.2 %convolution_convert_fusion = bf16[256,5120]{1,0:T(8,128)(2,1)} fusion(bf16[256,1024]{1,0:T(8,128)(2,1)S(1)} %fusion.4, bf16[5120,1024]{1,0:T(8,128)(2,1)} %all-gather.2.cloned.1.call-done), kind=kOutput, calls=%fused_computation.4 | convolution fusion | flops 2685665280 | bytes 13631488 | tf_op jit(solution)/shard_map/dot_general | solution.py:24
  836.5 57.8 %all-reduce.3.cloned.1.call-done = (f32[320,256]{0,1:T(8,128)}, f32[320,256]{0,1:T(8,128)}, f32[320,256]{0,1:T(8,128)}, f32[320,256]{0,1:T(8,128)}) async-done(((f32[320,256]{0,1:T(8,128)}, f32[320,256]{0,1:T(8,128)}, f32[320,256]{0,1:T(8,128)}, f32[320,256]{0,1:T(8,128)}), (f32[320,256]{0,1:T(8,128)}, f32[320,256]{0,1:T(8,128)}, f32[320,256]{0,1:T(8,128)}, ...) | async-done | bytes 1310736 | tf_op jit(solution)/shard_map/psum | solution.py:43
  894.3 2.6 maximum_multiply_fusion
  896.9 2.9 copy.8
  (2 shorter events, 0.0 us)
Async XLA Ops:
  7.2 231.1 %copy-start = (bf16[256,5120]{1,0:T(8,128)(2,1)S(1)}, bf16[256,5120]{1,0:T(8,128)(2,1)}, u32[]{:S(2)}) copy-start(bf16[256,5120]{1,0:T(8,128)(2,1)} %param.4) | copy-start | bytes 7864324
  7.2 231.0 %all-gather.2.cloned.1.call-start = ((), (), s32[]{:S(2)}) async-start(), calls=%async_computation.4 | async-start | bytes 11141120 | tf_op jit(solution)/shard_map/all_gather | solution.py:15
  7.9 236.1 %copy-start.1 = (bf16[256,1024]{1,0:T(8,128)(2,1)S(1)}, bf16[256,1024]{1,0:T(8,128)(2,1)}, u32[]{:S(2)}) copy-start(bf16[256,1024]{1,0:T(8,128)(2,1)} %param.7) | copy-start | bytes 1572868
  7.9 236.1 %copy-start.3 = (f32[1024]{0:T(1024)S(1)}, f32[1024]{0:T(1024)}, u32[]{:S(2)}) copy-start(f32[1024]{0:T(1024)} %param.6) | copy-start | bytes 12292
  7.9 366.3 %reduce-scatter.19.cloned.1.call-start = ((), (), s32[]{:S(2)}) async-start(), calls=%async_computation.8 | async-start | bytes 5570560
  238.2 6.2 copy-start.2
  253.8 243.4 %reduce-scatter.17.cloned.1.call-start = ((), (), s32[]{:S(2)}) async-start(), calls=%async_computation.7 | async-start | bytes 5570560
  262.9 356.9 %reduce-scatter.15.cloned.1.call-start = ((), (), s32[]{:S(2)}) async-start(), calls=%async_computation.6 | async-start | bytes 5570560
  272.2 470.3 %reduce-scatter.13.cloned.1.call-start = ((), (), s32[]{:S(2)}) async-start(), calls=%async_computation.5 | async-start | bytes 5570560
  281.4 612.9 %all-reduce.3.cloned.1.call-start = ((), (), s32[]{:S(2)}) async-start(), calls=%async_computation.9 | async-start | bytes 3145728 | tf_op jit(solution)/shard_map/psum | solution.py:43
Sparse Core Ops, SparseCore 0:
  9.8 228.3 all-gather.1
  253.9 120.3 reduce-scatter.18
  376.8 120.2 reduce-scatter.16
  499.5 120.2 reduce-scatter.14
  622.2 120.2 reduce-scatter.12
  745.9 148.3 all-reduce.2
where the time goes:
time: 907 us
  waiting for transfers between devices  744 us (82%)
  blocking collectives  79.2 us (9%)
  local copies, waits for them, and re-layouts  34.2 us (4%)
  matrix products  30.7 us (3%)
  between operations  14.2 us (2%)
    unnamed x10, waiting for transfers between devices  456 us
    all_gather x1, waiting for transfers between devices, per_device(): gathered = lax.all_gather(key_weight, 'shard', axis=0, tiled=True)  230 us
    psum x1, blocking collectives, per_device(): grad_gain = lax.psum(gain_part, ('rep', 'shard')) / devices  79.2 us
    psum x1, waiting for transfers between devices, per_device(): owned = lax.psum(owned, 'rep')  57.8 us
    unnamed x17, local copies, waits for them, and re-layouts  34.2 us
  transfers between devices with their start and end apart: 6, of which 6 were waited for; matrix products, arithmetic and copies ran while one was open for 5% of the time, Pallas kernels for 0%

commit v1 on v0

v1 whole, which is shorter than its diff:
```python
import jax
import jax.numpy as jnp
from jax import lax
from jax.experimental import pallas as pl
from jax.experimental.pallas import tpu as pltpu
from jax.sharding import PartitionSpec as P

MESH = pl.DeviceIdType.MESH
F32 = jnp.float32
BF16 = jnp.bfloat16

ROWS = 320
PAIR = 640
COLS = 512
TOK = 256
CR = 192
CH = 96
AQ = 32
AH = 16
OFFS = (0, 1, -1, 2, -2, 3, -3, 4)
POS = {off: i for i, off in enumerate(OFFS)}
DEVICES = 256


def aligned(value, to):
    return pl.multiple_of(value, to)


def kernel(
    tok_ref, w_ref, gain_ref, cot_ref,
    gt_ref, gw_ref, gg_ref,
    W, X, COT, ACC, GK, ST, STR,
    G, XR, YR, ZR, SB, AX, TH, FO,
    TS, TR, TM, TO, GB, GR,
    lsem, *sems,
):
    rep, shard = lax.axis_index("rep"), lax.axis_index("shard")
    x, h, c = rep // 4, (rep // 2) % 2, rep % 2
    z, p = shard // 2, shard % 2
    y = 2 * h + p

    def dev(dx=0, dy=0, dz=0, core=None):
        xx, yy, zz = (x + dx) % 4, (y + dy) % 4, (z + dz) % 8
        cc = c if core is None else core
        return {"rep": xx * 4 + (yy // 2) * 2 + cc, "shard": zz * 2 + yy % 2}

    sibling = dev(core=1 - c)
    y_xor1 = dev(dy=1 - 2 * (y % 2))
    x_xor1 = dev(dx=1 - 2 * (x % 2))
    z_xor1 = dev(dz=1 - 2 * (z % 2))
    z_xor2 = dev(dz=2 - 4 * ((z // 2) % 2))
    z_xor4 = dev(dz=4)

    def zo(pos):
        return (z + OFFS[pos] + 8) % 8

    counters = {}
    open_sends = []

    def remote(group, src, dst, to):
        ss, rs = sems[2 * GROUPS.index(group)], sems[2 * GROUPS.index(group) + 1]
        i = counters.get(group, 0)
        counters[group] = i + 1
        assert i < SEMS[group], group
        return pltpu.make_async_remote_copy(
            src_ref=src, dst_ref=dst, send_sem=ss.at[i], recv_sem=rs.at[i],
            device_id=to, device_id_type=MESH,
        )

    def send(copy):
        copy.start()
        open_sends.append(copy)

    lcount = [0]

    def local(src, dst):
        i = lcount[0]
        lcount[0] += 1
        copy = pltpu.make_async_copy(src, dst, lsem.at[i])
        copy.start()
        return copy

    my_cols = pl.ds(aligned(c * COLS, COLS), COLS)
    sib_cols = pl.ds(aligned((1 - c) * COLS, COLS), COLS)
    my_toks = pl.ds(aligned(c * TOK, TOK), TOK)
    sib_toks = pl.ds(aligned((1 - c) * TOK, TOK), TOK)

    w_load = local(w_ref.at[:, my_cols], W.at[z, p])
    loads = [local(cot_ref.at[:, my_cols], COT.at[my_toks])]
    for q in range(8):
        loads.append(local(tok_ref.at[:, pl.ds(q * PAIR, PAIR)], X.at[q, my_toks]))

    partners = [dev(dx=1), dev(dx=2), dev(dx=3), dev(dy=1), dev(dy=2), dev(dy=3),
                dev(dz=1), dev(dz=7), z_xor2, z_xor4, sibling]
    barrier = pltpu.get_barrier_semaphore()
    for to in partners:
        pl.semaphore_signal(barrier, inc=1, device_id=to, device_id_type=MESH)
    pl.semaphore_wait(barrier, len(partners))

    crow = [pl.ds(k * CH, CH) for k in range(2)]
    arow = [pl.ds(aligned(CR + x * AQ + k * AH, AH), AH) for k in range(2)]
    axq = pl.ds(aligned(CR + x * AQ, AQ), AQ)
    zcp = {}
    ycp = {}
    xcp = {}

    def zsend(sig, d, k):
        at = zo(POS[-sig * (d - 1)] if d > 1 else 0)
        for part, rows in (("c", crow[k]), ("a", arow[k])):
            copy = remote("gz", W.at[at, p, rows], W.at[at, p, rows], dev(dz=sig % 8))
            zcp[sig, d, k, part] = copy
            send(copy)

    def zwait(sig, d, k):
        for part in ("c", "a"):
            zcp[sig, d, k, part].wait_recv()

    def ysend(pos, k):
        at = zo(pos)
        for part, rows in (("c", crow[k]), ("a", arow[k])):
            copy = remote("gy", W.at[at, p, rows], W.at[at, p, rows], dev(dy=1 if k == 0 else 3))
            ycp[pos, k, part] = copy
            send(copy)

    def ywait(pos):
        for k in range(2):
            for part in ("c", "a"):
                ycp[pos, k, part].wait_recv()

    def xsend(pos):
        at = zo(pos)
        for j in (1, 3, 2):
            if pos == 0:
                ref = W.at[at, pl.ds(1 - p, 1), axq]
            else:
                ref = W.at[at, :, axq]
            copy = remote("gx", ref, ref, dev(dx=j))
            xcp[pos, j] = copy
            send(copy)

    def xwait(pos):
        for j in (1, 3, 2):
            xcp[pos, j].wait_recv()

    def project(pos, first=False):
        at = zo(pos)

        @pl.loop(0, 2)
        def _(i):
            rows = pl.ds(aligned(i * TOK, TOK), TOK)
            part = jnp.dot(X[at, rows], W[at].reshape(PAIR, COLS), preferred_element_type=F32)
            if first:
                ACC[rows] = part
            else:
                ACC[rows] += part

    w_load.wait()
    zsend(1, 1, 0)
    zsend(-1, 1, 1)
    ysend(0, 0)
    ysend(0, 1)
    zsend(1, 1, 1)
    zsend(-1, 1, 0)
    swaps = [remote("swap", cot_ref.at[:, sib_cols], COT.at[my_toks], sibling)]
    for q in range(8):
        swaps.append(remote("swap", tok_ref.at[:, pl.ds(q * PAIR, PAIR)], X.at[q, my_toks], sibling))
    for copy in swaps:
        send(copy)

    def at_distance(d):
        return [0] if d == 0 else [7] if d == 4 else [POS[d], POS[-d]]

    for d in range(1, 7):
        if d <= 4:
            for j in range(2):
                for sig in (1, -1):
                    k = j if sig == 1 else 1 - j
                    if d == 4 and j == 1:
                        continue
                    zwait(sig, d, k)
                    if d < 3 or (d == 3 and j == 0):
                        zsend(sig, d + 1, k)
                    ysend(POS[-sig * d] if d < 4 else 7, k)
        if d - 1 <= 4:
            for pos in at_distance(d - 1):
                ywait(pos)
                xsend(pos)
        if d == 2:
            for copy in loads:
                copy.wait()
            for copy in swaps:
                copy.wait_recv()
        if d >= 2:
            for pos in at_distance(d - 2):
                xwait(pos)
                project(pos, first=pos == 0)

    gain = gain_ref[0:1, my_cols]

    @pl.loop(0, 4)
    def _(i):
        rows = pl.ds(aligned(i * 128, 128), 128)
        proj = ACC[rows]
        scaled = COT[rows].astype(F32) * gain
        ssq = jnp.sum(proj * proj, axis=1, keepdims=True)
        sdot = jnp.sum(scaled * proj, axis=1, keepdims=True)
        lane = lax.broadcasted_iota(jnp.int32, (128, 128), 1)
        ST[rows] = jnp.where(lane < 64, ssq, sdot)

    stats = remote("stat", ST, STR, sibling)
    stats.start()
    stats.wait()
    GB[0] = jnp.zeros((8, COLS), F32)

    @pl.loop(0, 4)
    def _(i):
        rows = pl.ds(aligned(i * 128, 128), 128)
        both = ST[rows] + STR[rows]
        ssq = both[:, 0:1] * (1.0 / (2 * COLS))
        sdot = both[:, 64:65] * (1.0 / (2 * COLS))
        inverse = lax.rsqrt(ssq + 1e-06)
        normed = ACC[rows] * inverse
        cot = COT[rows].astype(F32)
        scaled = cot * gain
        GK[rows] = (inverse * (scaled - normed * (inverse * sdot))).astype(BF16)
        GB[0] += jnp.broadcast_to(jnp.sum(cot * normed, axis=0, keepdims=True), (8, COLS))

    rxc, ryc, rza = {}, {}, {}
    other = 1 - p

    def s1(pos):
        at = zo(pos)
        G[at] = lax.dot_general(
            X[at], GK[...], (((0,), (0,)), ((), ())), preferred_element_type=F32
        ).astype(BF16).reshape(2, ROWS, COLS)
        for j in (1, 3, 2):
            rows = pl.ds(aligned(CR + ((x + j) % 4) * AQ, AQ), AQ)
            copy = remote("rx", G.at[at, :, rows], XR.at[pos, j - 1], dev(dx=j))
            rxc[pos, j] = copy
            send(copy)
        for k in range(2):
            copy = remote("ry", G.at[at, other, crow[k]], YR.at[pos, crow[k]], dev(dy=1 if k == 0 else 3))
            ryc[pos, k, "c"] = copy
            send(copy)

    def s2(pos):
        at = zo(pos)
        for j in (1, 3, 2):
            rxc[pos, j].wait_recv()
        for parity in range(2):
            total = G[at, parity, axq].astype(F32)
            for j in range(3):
                total = total + XR[pos, j, parity].astype(F32)
            G[at, parity, axq] = total.astype(BF16)
        for k in range(2):
            copy = remote("ry", G.at[at, other, arow[k]], YR.at[pos, pl.ds(CR + k * AH, AH)], dev(dy=1 if k == 0 else 3))
            ryc[pos, k, "a"] = copy
            send(copy)

    def s3(pos):
        for k in range(2):
            for part in ("c", "a"):
                ryc[pos, k, part].wait_recv()

    def halves_of(sig, d):
        return ([0] if sig == 1 else [1]) if d == 4 else ([0, 1] if sig == 1 else [1, 0])

    def s4(pos, sig):
        d = abs(OFFS[pos])
        at = zo(pos)
        for k in halves_of(sig, d):
            came = d < 3 or (d == 3 and k == (0 if sig == 1 else 1))
            for part, rows, buf in (("c", crow[k], crow[k]), ("a", arow[k], pl.ds(CR + k * AH, AH))):
                total = G[at, p, rows].astype(F32) + YR[pos, buf].astype(F32)
                if came:
                    rza[sig, d, k, part].wait_recv()
                    total = total + ZR[0 if sig == 1 else 1, d, buf].astype(F32)
                G[at, p, rows] = total.astype(BF16)
                copy = remote("rz", G.at[at, p, rows], ZR.at[0 if sig == 1 else 1, d - 1, buf], dev(dz=sig % 8))
                rza[sig, d - 1, k, part] = copy
                send(copy)

    gtc = {}
    outs = []

    def gt(pos):
        at = zo(pos)
        weight = W[at].reshape(PAIR, COLS)
        TS[pos] = lax.dot_general(
            GK[sib_toks], weight, (((1,), (1,)), ((), ())), preferred_element_type=F32
        ).astype(BF16)
        copy = remote("gt", TS.at[pos], TR.at[pos], sibling)
        gtc[pos] = copy
        send(copy)
        TM[pos] = lax.dot_general(
            GK[my_toks], weight, (((1,), (1,)), ((), ())), preferred_element_type=F32
        )

    def gt_end(pos):
        gtc[pos].wait_recv()
        TO[pos] = (TM[pos] + TR[pos].astype(F32)).astype(BF16)
        outs.append(local(TO.at[pos], gt_ref.at[:, pl.ds(aligned(zo(pos) * PAIR, 128), PAIR)]))

    gains = [x_xor1, dev(dx=2), y_xor1, dev(dy=2), z_xor1, z_xor2, z_xor4]
    ggc = {}

    def gain_send(i):
        ggc[i] = remote("gg", GB.at[i], GR.at[i], gains[i])
        send(ggc[i])

    def gain_add(i):
        ggc[i].wait_recv()
        GB[i + 1] = GB[i] + GR[i]

    def gain_step(i):
        gain_add(i)
        if i + 1 < len(gains):
            gain_send(i + 1)

    gain_send(0)
    s1(7)
    s1(5)
    s1(6)
    s2(7)
    s1(3)
    s1(4)
    s3(7)
    s4(7, 1)
    s4(7, -1)
    s2(5)
    s2(6)
    gain_step(0)
    s1(1)
    s1(2)
    s1(0)
    s3(5)
    s4(5, 1)
    s3(6)
    s4(6, -1)
    s2(3)
    s2(4)
    gain_step(1)
    gt(7)
    gt(5)
    gt(6)
    gt_end(7)
    s3(3)
    s4(3, 1)
    s3(4)
    s4(4, -1)
    s2(1)
    s2(2)
    gain_step(2)
    gt(3)
    gt(4)
    gt_end(5)
    gt_end(6)
    gain_step(3)
    s3(1)
    s4(1, 1)
    s3(2)
    s4(2, -1)
    s2(0)
    gain_step(4)
    gt(1)
    gt(2)
    gt(0)
    gt_end(3)
    gt_end(4)
    gain_step(5)
    gt_end(1)
    gt_end(2)
    gt_end(0)
    gain_step(6)
    GB[0 + 8] = GB[7] * (1.0 / DEVICES)
    gg_out = [local(GB.at[8], gg_ref.at[:, my_cols])]
    gg_far = remote("go", GB.at[8], gg_ref.at[:, my_cols], sibling)
    send(gg_far)

    s3(0)
    for sig in (1, -1):
        for k in halves_of(sig, 0):
            for part in ("c", "a"):
                rza[sig, 0, k, part].wait_recv()
    mine = YR[0, 0:CR].astype(F32) + G[z, p, 0:CR].astype(F32)
    mine = mine + ZR[0, 0, 0:CR].astype(F32) + ZR[1, 0, 0:CR].astype(F32)
    SB[...] = mine.astype(BF16)
    QC = CR // 4
    axc = {}
    for j in (1, 3, 2):
        rows = pl.ds(aligned(((x + j) % 4) * QC, 16), QC)
        axc[j] = remote("ax", SB.at[rows], AX.at[j - 1], dev(dx=j))
        send(axc[j])
    last = G[z, p, axq].astype(F32) + YR[0, CR:].astype(F32)
    TH[0, QC:] = last + ZR[0, 0, CR:].astype(F32) + ZR[1, 0, CR:].astype(F32)
    for j in (1, 3, 2):
        axc[j].wait_recv()
    total = SB[pl.ds(aligned(x * QC, 16), QC)].astype(F32)
    for j in range(3):
        total = total + AX[j].astype(F32)
    TH[0, 0:QC] = total
    swap_h = remote("ah", TH.at[0], TH.at[1], dev(dy=2))
    send(swap_h)
    swap_h.wait_recv()
    crows = pl.ds(aligned(x * QC, 16), QC)
    FO[crows] = (TH[0, 0:QC] + TH[1, 0:QC]) * (1.0 / DEVICES)
    FO[axq] = (TH[0, QC:] + TH[1, QC:]) * (1.0 / DEVICES)
    fin = []
    for j in (1, 3, 2):
        for rows in (crows, axq):
            copy = remote("af", FO.at[rows], FO.at[rows], dev(dx=j))
            fin.append(copy)
            send(copy)
    for copy in fin:
        copy.wait_recv()
    gw_out = local(FO, gw_ref.at[:, my_cols])
    gw_far = remote("go", FO, gw_ref.at[:, my_cols], sibling)
    send(gw_far)
    gw_far.wait_recv()
    gg_far.wait_recv()
    gw_out.wait()
    for copy in gg_out + outs:
        copy.wait()
    for copy in open_sends:
        copy.wait_send()


SEMS = {"gz": 28, "gy": 32, "gx": 24, "swap": 9, "stat": 1, "rx": 24, "ry": 32, "rz": 28, "gt": 8, "gg": 7,
        "go": 2, "ax": 3, "ah": 1, "af": 6}
GROUPS = tuple(SEMS)


def per_device(tokens, key_weight, key_gain, key_cotangent):
    anywhere = pl.BlockSpec(memory_space=pl.ANY)
    vmem = pl.BlockSpec(memory_space=pltpu.VMEM)
    sems = []
    for group in GROUPS:
        sems += [pltpu.SemaphoreType.DMA((SEMS[group],))] * 2
    V = pltpu.VMEM
    grad_tokens, grad_weight, grad_gain = pl.pallas_call(
        kernel,
        out_shape=(
            jax.ShapeDtypeStruct((TOK, 5120), BF16),
            jax.ShapeDtypeStruct((ROWS, 1024), F32),
            jax.ShapeDtypeStruct((8, 1024), F32),
        ),
        in_specs=[anywhere, anywhere, vmem, anywhere],
        out_specs=(anywhere, anywhere, anywhere),
        scratch_shapes=[
            V((8, 2, ROWS, COLS), BF16),
            V((8, 2 * TOK, PAIR), BF16),
            V((2 * TOK, COLS), BF16),
            V((2 * TOK, COLS), F32),
            V((2 * TOK, COLS), BF16),
            V((2 * TOK, 128), F32),
            V((2 * TOK, 128), F32),
            V((8, 2, ROWS, COLS), BF16),
            V((8, 3, 2, AQ, COLS), BF16),
            V((8, CR + AQ, COLS), BF16),
            V((2, 4, CR + AQ, COLS), BF16),
            V((CR, COLS), BF16),
            V((3, CR // 4, COLS), BF16),
            V((2, ROWS // 4, COLS), F32),
            V((ROWS, COLS), F32),
            V((8, TOK, PAIR), BF16),
            V((8, TOK, PAIR), BF16),
            V((8, TOK, PAIR), F32),
            V((8, TOK, PAIR), BF16),
            V((9, 8, COLS), F32),
            V((7, 8, COLS), F32),
            pltpu.SemaphoreType.DMA((24,)),
            *sems,
        ],
        compiler_params=pltpu.CompilerParams(
            collective_id=0, has_side_effects=True, vmem_limit_bytes=60 * 2**20
        ),
        name="key_projection_backward",
    )(tokens, key_weight, key_gain.reshape(1, 1024), key_cotangent)
    return grad_tokens, grad_weight, grad_gain[0]


def solution(mesh):
    return jax.shard_map(
        per_device,
        mesh=mesh,
        in_specs=(P(("rep", "shard"), None), P("shard", None), P(), P(("rep", "shard"), None)),
        out_specs=(P(("rep", "shard"), None), P("shard", None), P()),
        check_vma=False,
    )
```

time: 907 us -> 116 us (0.13)
  waiting for transfers between devices: 744 us -> 0 us
  Pallas kernels: 0 us -> 110 us
  blocking collectives: 79.2 us -> 0 us
  matrix products: 30.7 us -> 0 us
  local copies, waits for them, and re-layouts: 34.2 us -> 5.92 us
  between operations: 14.2 us -> 0.64 us
    unnamed x10 -> x0, waiting for transfers between devices: 456 us -> none
    all_gather x1 -> x0, waiting for transfers between devices: 230 us -> none  [per_device(): gathered = lax.all_gather(key_weight, 'shard', axis=0, tiled=True)]
    pallas_call x0 -> x1, Pallas kernels: none -> 110 us  [per_device(): pl.pallas_call(kernel, out_shape=(jax.ShapeDtypeStruct((TOK, 5120), BF16)...]
    psum x1 -> x0, blocking collectives: 79.2 us -> none  [per_device(): grad_gain = lax.psum(gain_part, ('rep', 'shard')) / devices]
    psum x1 -> x0, waiting for transfers between devices: 57.8 us -> none  [per_device(): owned = lax.psum(owned, 'rep')]
    dot_general x6 -> x0, matrix products: 30.7 us -> none  [the longest x4 12.8 us: term(): lax.dot_general(tokens, bucket_grad, (((0,), (0,)), ((), ())), preferred_...]
    unnamed x17 -> x4, local copies, waits for them, and re-layouts: 34.2 us -> 4.56 us
  transfers between devices with their start and end apart: 6 -> 0, of which waited for: 6 -> 0; matrix products, arithmetic and copies ran while one was open for 5% -> 0% of each run, Pallas kernels for 0% -> 0%
where the time goes in v1:
time: 116 us
  Pallas kernels  110 us (95%)
  local copies, waits for them, and re-layouts  5.92 us (5%)
    pallas_call x1, Pallas kernels, per_device(): pl.pallas_call(kernel, out_shape=(jax.ShapeDtypeStruct((TOK, 5120), BF16)...  110 us
    unnamed x4, local copies, waits for them, and re-layouts  4.56 us

profile of v1, /device:TPU:1, one launch (start us, length us, event | category | flops | bytes accessed | tf_op | source)
XLA Modules:
  0.0 116.2 jit_solution(2863439492130447469)
XLA Ops:
  0.6 109.7 %key_projection_backward.1 = (bf16[256,5120]{1,0:T(8,128)(2,1)}, f32[320,1024]{1,0:T(8,128)}, f32[8,1024]{1,0:T(8,128)}) custom-call(bf16[256,5120]{1,0:T(8,128)(2,1)} %tok_ref.1, bf16[320,1024]{1,0:T(8,128)(2,1)} %w_ref.1, f32[1,1024]{1,0:T(1,128)} %bitcast.2, bf16[256,1024]{1,0:T(8,128)(2,1)} %cot_ref.1), custom_call_target="tpu_custom_call" | custom-call | tf_op jit(solution)/shard_map/key_projection_backward/pallas_call | solution.py:440
  110.3 1.4 %slice.3 = f32[1,1024]{1,0:T(1,128)} slice(f32[8,1024]{1,0:T(8,128)} %get-tuple-element.8), slice={[0:1], [0:1024]} | slice | bytes 8192 | tf_op jit(solution)/shard_map/slice | solution.py:479
  111.7 0.0 copy-start
  111.7 3.5 %copy.9 = bf16[256,5120]{1,0:T(8,128)(2,1)} copy(bf16[256,5120]{1,0:T(8,128)(2,1)} %get-tuple-element.12) | data formatting | bytes 5242880
  115.2 0.0 copy-done
  115.2 1.1 copy.10
Async XLA Ops:
  111.7 3.5 %copy-start = (f32[320,1024]{1,0:T(8,128)S(1)}, f32[320,1024]{1,0:T(8,128)}, u32[]{:S(2)}) copy-start(f32[320,1024]{1,0:T(8,128)} %get-tuple-element.13) | copy-start | bytes 3932164

commit v2 on v1

v2 whole, which is shorter than its diff:
```python
import jax
import jax.numpy as jnp
from jax import lax
from jax.experimental import pallas as pl
from jax.experimental.pallas import tpu as pltpu
from jax.sharding import PartitionSpec as P

MESH = pl.DeviceIdType.MESH
F32 = jnp.float32
BF16 = jnp.bfloat16

ROWS = 320
PAIR = 640
COLS = 512
TOK = 256
CR = 192
CH = 96
AQ = 32
AH = 16
OFFS = (0, 1, -1, 2, -2, 3, -3, 4)
POS = {off: i for i, off in enumerate(OFFS)}
DEVICES = 256
THT = F32


def aligned(value, to):
    return pl.multiple_of(value, to)


def kernel(
    tok_ref, w_ref, gain_ref, cot_ref,
    gt_ref, gw_ref, gg_ref,
    W, X, COT, ACC, GK, ST, STR,
    G, XR, YR, ZR, SB, AX, TH, FO,
    TS, TR, TM, TO, GB, GX, GY, GZ,
    lsem, *sems,
):
    rep, shard = lax.axis_index("rep"), lax.axis_index("shard")
    x, h, c = rep // 4, (rep // 2) % 2, rep % 2
    z, p = shard // 2, shard % 2
    y = 2 * h + p

    def dev(dx=0, dy=0, dz=0, core=None):
        xx, yy, zz = (x + dx) % 4, (y + dy) % 4, (z + dz) % 8
        cc = c if core is None else core
        return {"rep": xx * 4 + (yy // 2) * 2 + cc, "shard": zz * 2 + yy % 2}

    sibling = dev(core=1 - c)
    def zo(pos):
        return (z + OFFS[pos] + 8) % 8

    counters = {}
    open_sends = []

    def remote(group, src, dst, to):
        ss, rs = sems[2 * GROUPS.index(group)], sems[2 * GROUPS.index(group) + 1]
        i = counters.get(group, 0)
        counters[group] = i + 1
        assert i < SEMS[group], group
        return pltpu.make_async_remote_copy(
            src_ref=src, dst_ref=dst, send_sem=ss.at[i], recv_sem=rs.at[i],
            device_id=to, device_id_type=MESH,
        )

    def send(copy):
        copy.start()
        open_sends.append(copy)

    lcount = [0]

    def local(src, dst):
        i = lcount[0]
        lcount[0] += 1
        copy = pltpu.make_async_copy(src, dst, lsem.at[i])
        copy.start()
        return copy

    my_cols = pl.ds(aligned(c * COLS, COLS), COLS)
    sib_cols = pl.ds(aligned((1 - c) * COLS, COLS), COLS)
    my_toks = pl.ds(aligned(c * TOK, TOK), TOK)
    sib_toks = pl.ds(aligned((1 - c) * TOK, TOK), TOK)

    w_load = local(w_ref.at[:, my_cols], W.at[z, p])
    loads = [local(cot_ref.at[:, my_cols], COT.at[my_toks])]
    for q in range(8):
        loads.append(local(tok_ref.at[:, pl.ds(q * PAIR, PAIR)], X.at[q, my_toks]))

    partners = [dev(dx=i) for i in range(1, 4)] + [dev(dy=i) for i in range(1, 4)]
    partners += [dev(dz=i) for i in range(1, 8)] + [sibling]
    barrier = pltpu.get_barrier_semaphore()
    for to in partners:
        pl.semaphore_signal(barrier, inc=1, device_id=to, device_id_type=MESH)
    pl.semaphore_wait(barrier, len(partners))

    crow = [pl.ds(k * CH, CH) for k in range(2)]
    arow = [pl.ds(aligned(CR + x * AQ + k * AH, AH), AH) for k in range(2)]
    axq = pl.ds(aligned(CR + x * AQ, AQ), AQ)
    cp = {}

    def at_step(sig, d):
        return 0 if d == 0 else 7 if d == 4 else POS[-sig * d]

    def zc(sig, d, k):
        ref = W.at[zo(at_step(sig, d - 1)), p, crow[k]]
        cp["zc", sig, d, k] = remote("gz", ref, ref, dev(dz=sig % 8))
        send(cp["zc", sig, d, k])

    def za(sig, d):
        rows = axq if d < 4 else arow[0 if sig == 1 else 1]
        ref = W.at[zo(at_step(sig, d - 1)), p, rows]
        cp["za", sig, d] = remote("gz", ref, ref, dev(dz=sig % 8))
        send(cp["za", sig, d])

    def yc(pos, k):
        ref = W.at[zo(pos), p, crow[k]]
        cp["yc", pos, k] = remote("gy", ref, ref, dev(dy=1 if k == 0 else 3))
        send(cp["yc", pos, k])

    def ya(pos, k):
        ref = W.at[zo(pos), p, arow[k]]
        cp["ya", pos, k] = remote("gy", ref, ref, dev(dy=1 if k == 0 else 3))
        send(cp["ya", pos, k])

    def xs(pos):
        for j in (1, 3, 2):
            ref = W.at[zo(pos), pl.ds(1 - p, 1), axq] if pos == 0 else W.at[zo(pos), :, axq]
            cp["x", pos, j] = remote("gx", ref, ref, dev(dx=j))
            send(cp["x", pos, j])

    def got(*key):
        cp[key].wait_recv()

    def project(pos, first=False):
        at = zo(pos)

        @pl.loop(0, 2)
        def _(i):
            rows = pl.ds(aligned(i * TOK, TOK), TOK)
            part = jnp.dot(X[at, rows], W[at].reshape(PAIR, COLS), preferred_element_type=F32)
            if first:
                ACC[rows] = part
            else:
                ACC[rows] += part

    def positions(d):
        return [0] if d == 0 else [7] if d == 4 else [POS[d], POS[-d]]

    def a_step(d):
        for sig in (1, -1):
            got("za", sig, d)
            if d < 4:
                za(sig, d + 1)
                for k in range(2):
                    ya(at_step(sig, d), k)
            else:
                ya(7, 0 if sig == 1 else 1)

    def ax_step(d):
        for pos in positions(d):
            for k in range(2):
                got("ya", pos, k)
            xs(pos)

    def c_step(d, j):
        for sig in (1, -1):
            k = j if sig == 1 else 1 - j
            got("zc", sig, d, k)
            if d < 3 or (d == 3 and j == 0):
                zc(sig, d + 1, k)
            yc(at_step(sig, d), k)

    def finish(d):
        for pos in positions(d):
            for k in range(2):
                got("yc", pos, k)
            for j in (1, 3, 2):
                got("x", pos, j)
            project(pos, first=pos == 0)

    w_load.wait()
    za(1, 1)
    za(-1, 1)
    ya(0, 0)
    ya(0, 1)
    zc(1, 1, 0)
    zc(-1, 1, 1)
    yc(0, 0)
    yc(0, 1)
    swaps = [remote("swap", cot_ref.at[:, sib_cols], COT.at[my_toks], sibling)]
    for q in range(8):
        swaps.append(remote("swap", tok_ref.at[:, pl.ds(q * PAIR, PAIR)], X.at[q, my_toks], sibling))
    for copy in swaps:
        send(copy)
    a_step(1)
    zc(1, 1, 1)
    zc(-1, 1, 0)
    ax_step(0)
    c_step(1, 0)
    a_step(2)
    ax_step(1)
    c_step(1, 1)
    a_step(3)
    ax_step(2)
    a_step(4)
    c_step(2, 0)
    ax_step(3)
    c_step(2, 1)
    ax_step(4)
    for copy in loads:
        copy.wait()
    for copy in swaps:
        copy.wait_recv()
    c_step(3, 0)
    finish(0)
    c_step(3, 1)
    finish(1)
    c_step(4, 0)
    finish(2)
    finish(3)
    finish(4)

    gain = gain_ref[0:1, my_cols]

    @pl.loop(0, 4)
    def _(i):
        rows = pl.ds(aligned(i * 128, 128), 128)
        proj = ACC[rows]
        scaled = COT[rows].astype(F32) * gain
        ssq = jnp.sum(proj * proj, axis=1, keepdims=True)
        sdot = jnp.sum(scaled * proj, axis=1, keepdims=True)
        lane = lax.broadcasted_iota(jnp.int32, (128, 128), 1)
        ST[rows] = jnp.where(lane < 64, ssq, sdot)

    stats = remote("stat", ST, STR, sibling)
    stats.start()
    stats.wait()
    GX[x] = jnp.zeros((8, COLS), F32)

    @pl.loop(0, 4)
    def _(i):
        rows = pl.ds(aligned(i * 128, 128), 128)
        both = ST[rows] + STR[rows]
        ssq = both[:, 0:1] * (1.0 / (2 * COLS))
        sdot = both[:, 64:65] * (1.0 / (2 * COLS))
        inverse = lax.rsqrt(ssq + 1e-06)
        normed = ACC[rows] * inverse
        cot = COT[rows].astype(F32)
        scaled = cot * gain
        GK[rows] = (inverse * (scaled - normed * (inverse * sdot))).astype(BF16)
        GX[x] += jnp.broadcast_to(jnp.sum(cot * normed, axis=0, keepdims=True), (8, COLS))

    other = 1 - p
    half = [pl.ds(CR + k * AH, AH) for k in range(2)]

    def half_of(quarter, k):
        return pl.ds(aligned(CR + (quarter % 4) * AQ + k * AH, AH), AH)

    def partial(pos):
        G[zo(pos)] = lax.dot_general(
            X[zo(pos)], GK[...], (((0,), (0,)), ((), ())), preferred_element_type=F32
        ).astype(BF16).reshape(2, ROWS, COLS)

    def y_wide(pos):
        for k in range(2):
            cp["yw", pos, k] = remote("ry", G.at[zo(pos), other, crow[k]], YR.at[pos, crow[k]], dev(dy=1 if k == 0 else 3))
            send(cp["yw", pos, k])

    def x_first(pos):
        at = zo(pos)
        for way in range(2):
            step = 1 if way == 0 else 3
            rows = half_of(x + 2, way)
            cp["x1", pos, way] = remote("rx", G.at[at, :, rows], XR.at[pos, way, 0], dev(dx=step))
            send(cp["x1", pos, way])
            rows = half_of(x + step, 1 - way)
            cp["x2", pos, way] = remote("rx", G.at[at, :, rows], XR.at[pos, way, 1], dev(dx=step))
            send(cp["x2", pos, way])

    def x_second(pos):
        at = zo(pos)
        for way in range(2):
            step = 1 if way == 0 else 3
            rows = half_of(x + step, way)
            got("x1", pos, way)
            for parity in range(2):
                G[at, parity, rows] = (G[at, parity, rows].astype(F32) + XR[pos, way, 0, parity].astype(F32)).astype(BF16)
            cp["x3", pos, way] = remote("rx", G.at[at, :, rows], XR.at[pos, way, 2], dev(dx=step))
            send(cp["x3", pos, way])

    def x_third(pos):
        at = zo(pos)
        for way in range(2):
            got("x2", pos, way)
            got("x3", pos, way)
        for k in range(2):
            for parity in range(2):
                total = G[at, parity, arow[k]].astype(F32) + XR[pos, k, 2, parity].astype(F32)
                total = total + XR[pos, 1 - k, 1, parity].astype(F32)
                G[at, parity, arow[k]] = total.astype(BF16)
        for k in range(2):
            cp["yn", pos, k] = remote("ry", G.at[at, other, arow[k]], YR.at[pos, half[k]], dev(dy=1 if k == 0 else 3))
            send(cp["yn", pos, k])

    def owner(sig, d):
        return 0 if d == 0 else 7 if d == 4 else POS[sig * d]

    def first_half(sig):
        return 0 if sig == 1 else 1

    def z_sum(sig, d, k, rows, buf, name):
        pos, at, way = owner(sig, d), zo(owner(sig, d)), 0 if sig == 1 else 1
        got("y" + name, pos, k)
        total = G[at, p, rows].astype(F32) + YR[pos, buf].astype(F32)
        if d < 3 or (d == 3 and k == first_half(sig)):
            got("z" + name, sig, d, k)
            total = total + ZR[way, d, buf].astype(F32)
        G[at, p, rows] = total.astype(BF16)
        cp["z" + name, sig, d - 1, k] = remote("rz", G.at[at, p, rows], ZR.at[way, d - 1, buf], dev(dz=sig % 8))
        send(cp["z" + name, sig, d - 1, k])

    def z_wide(d, j):
        for sig in (1, -1):
            k = first_half(sig) if j == 1 else 1 - first_half(sig)
            z_sum(sig, d, k, crow[k], crow[k], "w")

    def z_narrow(d):
        for sig in (1, -1):
            for k in ([first_half(sig)] if d == 4 else [1 - first_half(sig), first_half(sig)]):
                z_sum(sig, d, k, arow[k], half[k], "n")

    gtc = {}
    outs = []

    def gt(pos):
        at = zo(pos)
        weight = W[at].reshape(PAIR, COLS)
        TS[pos] = lax.dot_general(
            GK[sib_toks], weight, (((1,), (1,)), ((), ())), preferred_element_type=F32
        ).astype(BF16)
        copy = remote("gt", TS.at[pos], TR.at[pos], sibling)
        gtc[pos] = copy
        send(copy)
        TM[pos] = lax.dot_general(
            GK[my_toks], weight, (((1,), (1,)), ((), ())), preferred_element_type=F32
        )

    def gt_end(pos):
        gtc[pos].wait_recv()
        TO[pos] = (TM[pos] + TR[pos].astype(F32)).astype(BF16)
        outs.append(local(TO.at[pos], gt_ref.at[:, pl.ds(aligned(zo(pos) * PAIR, 128), PAIR)]))

    def gain_send(name, buf, mine, hops):
        for hop in hops:
            cp["gain" + name, hop] = remote("gg", buf.at[mine], buf.at[mine], dev(**{"d" + name: hop}))
            send(cp["gain" + name, hop])

    def gain_sum(name, buf, hops):
        for hop in hops:
            got("gain" + name, hop)
        total = buf[0]
        for i in range(1, len(hops) + 1):
            total = total + buf[i]
        return total

    def gain_step(i):
        if i == 0:
            gain_send("x", GX, x, (1, 3, 2))
        elif i == 1:
            GY[y] = gain_sum("x", GX, (1, 3, 2))
            gain_send("y", GY, y, (1, 3, 2))
        elif i == 2:
            GZ[z] = gain_sum("y", GY, (1, 3, 2))
            gain_send("z", GZ, z, (1, 7, 2, 6, 3, 5, 4))
        else:
            GB[...] = gain_sum("z", GZ, (1, 7, 2, 6, 3, 5, 4)) * (1.0 / DEVICES)

    gain_step(0)
    partial(7)
    y_wide(7)
    x_first(7)
    partial(5)
    y_wide(5)
    partial(6)
    y_wide(6)
    x_first(5)
    x_first(6)
    partial(3)
    y_wide(3)
    partial(4)
    y_wide(4)
    z_wide(4, 1)
    x_second(7)
    partial(1)
    y_wide(1)
    z_wide(3, 0)
    x_first(3)
    partial(2)
    y_wide(2)
    x_second(5)
    x_third(7)
    x_first(4)
    partial(0)
    y_wide(0)
    z_wide(3, 1)
    x_second(6)
    x_third(5)
    x_first(1)
    z_wide(2, 0)
    x_second(3)
    x_third(6)
    z_narrow(4)
    x_first(2)
    gt(7)
    gain_step(1)
    z_wide(2, 1)
    x_second(4)
    x_third(3)
    x_first(0)
    gt(5)
    z_wide(1, 0)
    x_second(1)
    x_third(4)
    z_narrow(3)
    gt(6)
    gain_step(2)
    z_wide(1, 1)
    x_second(2)
    x_third(1)
    gt(3)
    z_narrow(2)
    x_second(0)
    x_third(2)
    gt(4)
    z_narrow(1)
    x_third(0)
    gt(1)
    gt(2)
    gt(0)
    QC = CR // 4
    for sig in (1, -1):
        for k in range(2):
            got("zw", sig, 0, k)
    for k in range(2):
        got("yw", 0, k)
    mine = YR[0, 0:CR].astype(F32) + G[z, p, 0:CR].astype(F32)
    mine = mine + ZR[0, 0, 0:CR].astype(F32) + ZR[1, 0, 0:CR].astype(F32)
    SB[...] = mine.astype(BF16)
    for j in (1, 3, 2):
        rows = pl.ds(aligned(((x + j) % 4) * QC, 16), QC)
        cp["ax", j] = remote("ax", SB.at[rows], AX.at[j - 1], dev(dx=j))
        send(cp["ax", j])
    for sig in (1, -1):
        for k in range(2):
            got("zn", sig, 0, k)
    for k in range(2):
        got("yn", 0, k)
    last = G[z, p, axq].astype(F32) + YR[0, CR:].astype(F32)
    TH[0, QC:] = (last + ZR[0, 0, CR:].astype(F32) + ZR[1, 0, CR:].astype(F32)).astype(TH.dtype)
    ah = [remote("ah", TH.at[0, pl.ds(QC, AQ)], TH.at[1, pl.ds(QC, AQ)], dev(dy=2))]
    send(ah[0])
    for q in (7, 5, 6, 3, 4, 1, 2, 0):
        gt_end(q)
    gain_step(3)
    gg_out = [local(GB, gg_ref.at[:, my_cols])]
    gg_far = remote("go", GB, gg_ref.at[:, my_cols], sibling)
    send(gg_far)

    for j in (1, 3, 2):
        got("ax", j)
    crows = pl.ds(aligned(x * QC, 16), QC)
    total = SB[crows].astype(F32)
    for j in range(3):
        total = total + AX[j].astype(F32)
    TH[0, 0:QC] = total.astype(TH.dtype)
    ah.append(remote("ah", TH.at[0, pl.ds(0, QC)], TH.at[1, pl.ds(0, QC)], dev(dy=2)))
    send(ah[1])
    fin = {}
    for i, rows, buf in ((0, axq, pl.ds(QC, AQ)), (1, crows, pl.ds(0, QC))):
        ah[i].wait_recv()
        FO[c, rows] = ((TH[0, buf].astype(F32) + TH[1, buf].astype(F32)) * (1.0 / DEVICES)).astype(BF16)
        for j in (1, 3, 2):
            fin[i, j] = remote("af", FO.at[c, rows], FO.at[c, rows], dev(dx=j))
            send(fin[i, j])
        fin[i, 0] = remote("ac", FO.at[c, rows], FO.at[c, rows], sibling)
        send(fin[i, 0])
    far = []
    for j in (1, 3, 2):
        source = (x + 4 - j) % 4
        for i, rows in ((0, pl.ds(aligned(CR + source * AQ, AQ), AQ)), (1, pl.ds(aligned(source * QC, 16), QC))):
            fin[i, j].wait_recv()
            copy = remote("ac", FO.at[c, rows], FO.at[c, rows], sibling)
            far.append(copy)
            send(copy)
    for copy in far + [fin[0, 0], fin[1, 0]]:
        copy.wait_recv()
    gw_out = local(FO, gw_ref)
    gg_far.wait_recv()
    gw_out.wait()
    for copy in gg_out + outs:
        copy.wait()
    for copy in open_sends:
        copy.wait_send()


def finish(gt_in, gw_in, gg_in, gt_ref, gw_ref, gg_ref, buf, sem):
    parts = [pl.ds(i * TOK // 4, TOK // 4) for i in range(4)]
    reads = [pltpu.make_async_copy(gt_in.at[rows], buf.at[rows], sem.at[0, i]) for i, rows in enumerate(parts)]
    writes = [pltpu.make_async_copy(buf.at[rows], gt_ref.at[rows], sem.at[1, i]) for i, rows in enumerate(parts)]
    for read in reads:
        read.start()
    for half in range(2):
        gw_ref[:, half * COLS : (half + 1) * COLS] = gw_in[half].astype(F32)
    gg_ref[...] = gg_in[0:1]
    for read, write in zip(reads, writes):
        read.wait()
        write.start()
    for write in writes:
        write.wait()


SEMS = {"gz": 30, "gy": 32, "gx": 24, "swap": 9, "stat": 1, "rx": 48, "ry": 32, "rz": 28, "gt": 8, "gg": 13,
        "go": 1, "ax": 3, "ah": 2, "af": 6, "ac": 8}
GROUPS = tuple(SEMS)


def per_device(tokens, key_weight, key_gain, key_cotangent):
    anywhere = pl.BlockSpec(memory_space=pl.ANY)
    vmem = pl.BlockSpec(memory_space=pltpu.VMEM)
    sems = []
    for group in GROUPS:
        sems += [pltpu.SemaphoreType.DMA((SEMS[group],))] * 2
    V = pltpu.VMEM
    grad_tokens, grad_weight, grad_gain = pl.pallas_call(
        kernel,
        out_shape=(
            jax.ShapeDtypeStruct((TOK, 5120), BF16),
            jax.ShapeDtypeStruct((2, ROWS, COLS), BF16),
            jax.ShapeDtypeStruct((8, 1024), F32),
        ),
        in_specs=[anywhere, anywhere, vmem, anywhere],
        out_specs=(anywhere, anywhere, anywhere),
        scratch_shapes=[
            V((8, 2, ROWS, COLS), BF16),
            V((8, 2 * TOK, PAIR), BF16),
            V((2 * TOK, COLS), BF16),
            V((2 * TOK, COLS), F32),
            V((2 * TOK, COLS), BF16),
            V((2 * TOK, 128), F32),
            V((2 * TOK, 128), F32),
            V((8, 2, ROWS, COLS), BF16),
            V((8, 2, 3, 2, AH, COLS), BF16),
            V((8, CR + AQ, COLS), BF16),
            V((2, 4, CR + AQ, COLS), BF16),
            V((CR, COLS), BF16),
            V((3, CR // 4, COLS), BF16),
            V((2, ROWS // 4, COLS), THT),
            V((2, ROWS, COLS), BF16),
            V((8, TOK, PAIR), BF16),
            V((8, TOK, PAIR), BF16),
            V((8, TOK, PAIR), F32),
            V((8, TOK, PAIR), BF16),
            V((8, COLS), F32),
            V((4, 8, COLS), F32),
            V((4, 8, COLS), F32),
            V((8, 8, COLS), F32),
            pltpu.SemaphoreType.DMA((24,)),
            *sems,
        ],
        compiler_params=pltpu.CompilerParams(
            collective_id=0, has_side_effects=True, vmem_limit_bytes=60 * 2**20
        ),
        name="key_projection_backward",
    )(tokens, key_weight, key_gain.reshape(1, 1024), key_cotangent)
    grad_tokens, grad_weight, grad_gain = pl.pallas_call(
        finish,
        out_shape=(
            jax.ShapeDtypeStruct((TOK, 5120), BF16),
            jax.ShapeDtypeStruct((ROWS, 1024), F32),
            jax.ShapeDtypeStruct((1, 1024), F32),
        ),
        in_specs=[anywhere, vmem, vmem],
        out_specs=(anywhere, vmem, vmem),
        scratch_shapes=[pltpu.VMEM((TOK, 5120), BF16), pltpu.SemaphoreType.DMA((2, 4))],
        name="write_results",
    )(grad_tokens, grad_weight, grad_gain)
    return grad_tokens, grad_weight, grad_gain.reshape(1024)


def solution(mesh):
    return jax.shard_map(
        per_device,
        mesh=mesh,
        in_specs=(P(("rep", "shard"), None), P("shard", None), P(), P(("rep", "shard"), None)),
        out_specs=(P(("rep", "shard"), None), P("shard", None), P()),
        check_vma=False,
    )
```

time: 116 us -> 103 us (0.89)
  Pallas kernels: 110 us -> 102 us
  local copies, waits for them, and re-layouts: 5.92 us -> 0 us
    pallas_call x1, Pallas kernels: 110 us -> 97.1 us  [per_device(): pl.pallas_call(kernel, out_shape=(jax.ShapeDtypeStruct((TOK, 5120), BF16)...]
    pallas_call x0 -> x1, Pallas kernels: none -> 4.79 us  [per_device(): pl.pallas_call(finish, out_shape=(jax.ShapeDtypeStruct((TOK, 5120), BF16)...]
    unnamed x4 -> x0, local copies, waits for them, and re-layouts: 4.56 us -> none
    slice x1 -> x0, local copies, waits for them, and re-layouts: 1.35 us -> none  [per_device(): return (grad_tokens, grad_weight, grad_gain[0])]
where the time goes in v2:
time: 103 us
  Pallas kernels  102 us (99%)
    pallas_call x1, Pallas kernels, per_device(): pl.pallas_call(kernel, out_shape=(jax.ShapeDtypeStruct((TOK, 5120), BF16)...  97.1 us
    pallas_call x1, Pallas kernels, per_device(): pl.pallas_call(finish, out_shape=(jax.ShapeDtypeStruct((TOK, 5120), BF16)...  4.79 us

profile of v2, /device:TPU:1, one launch (start us, length us, event | category | flops | bytes accessed | tf_op | source)
XLA Modules:
  0.0 102.7 jit_solution(16250894270799215767)
XLA Ops:
  0.6 97.1 %key_projection_backward.1 = (bf16[256,5120]{1,0:T(8,128)(2,1)}, bf16[2,320,512]{2,1,0:T(8,128)(2,1)}, f32[8,1024]{1,0:T(8,128)}) custom-call(bf16[256,5120]{1,0:T(8,128)(2,1)} %tok_ref.1, bf16[320,1024]{1,0:T(8,128)(2,1)} %w_ref.1, f32[1,1024]{1,0:T(1,128)} %bitcast.2, bf16[256,1024]{1,0:T(8,128)(2,1)} %cot_ref.1), custom_call_target="tpu_custom_call" | custom-call | tf_op jit(solution)/shard_map/key_projection_backward/pallas_call | solution.py:533
  97.8 4.8 %write_results.1 = (bf16[256,5120]{1,0:T(8,128)(2,1)}, f32[320,1024]{1,0:T(8,128)}, f32[1,1024]{1,0:T(1,128)}) custom-call(bf16[256,5120]{1,0:T(8,128)(2,1)} %get-tuple-element.9.gt_in, bf16[2,320,512]{2,1,0:T(8,128)(2,1)} %get-tuple-element.10.gw_in, f32[8,1024]{1,0:T(8,128)} %get-tuple-element.11.gg_in), custom_call_target="tpu_custom_call" | custom-call | tf_op jit(solution)/shard_map/write_results/pallas_call | solution.py:574

commit v3 on v2

v3 whole, which is shorter than its diff:
```python
import jax
import jax.numpy as jnp
from jax import lax
from jax.experimental import pallas as pl
from jax.experimental.pallas import tpu as pltpu
from jax.sharding import PartitionSpec as P

MESH = pl.DeviceIdType.MESH
F32 = jnp.float32
BF16 = jnp.bfloat16

ROWS = 320
PAIR = 640
COLS = 512
TOK = 256
CR = 192
CH = 96
AQ = 32
AH = 16
OFFS = (0, 1, -1, 2, -2, 3, -3, 4)
POS = {off: i for i, off in enumerate(OFFS)}
DEVICES = 256


def aligned(value, to):
    return pl.multiple_of(value, to)


def kernel(
    tok_ref, w_ref, gain_ref, cot_ref,
    gt_ref, gw_ref, gg_ref,
    W, X, COT, ACC, GK, ST, STR,
    G, XR, YR, ZR, SB, SF, AX, NB, NR, FO,
    TS, TR, TM, GB, GX, GY, GZ,
    lsem, *sems,
):
    rep, shard = lax.axis_index("rep"), lax.axis_index("shard")
    x, h, c = rep // 4, (rep // 2) % 2, rep % 2
    z, p = shard // 2, shard % 2
    y = 2 * h + p

    def dev(dx=0, dy=0, dz=0, core=None):
        xx, yy, zz = (x + dx + 4) % 4, (y + dy) % 4, (z + dz) % 8
        cc = c if core is None else core
        return {"rep": xx * 4 + (yy // 2) * 2 + cc, "shard": zz * 2 + yy % 2}

    sibling = dev(core=1 - c)
    def zo(pos):
        return (z + OFFS[pos] + 8) % 8

    counters = {}
    open_sends = []

    def remote(group, src, dst, to):
        ss, rs = sems[2 * GROUPS.index(group)], sems[2 * GROUPS.index(group) + 1]
        i = counters.get(group, 0)
        counters[group] = i + 1
        assert i < SEMS[group], group
        return pltpu.make_async_remote_copy(
            src_ref=src, dst_ref=dst, send_sem=ss.at[i], recv_sem=rs.at[i],
            device_id=to, device_id_type=MESH,
        )

    def send(copy):
        copy.start()
        open_sends.append(copy)

    lcount = [0]

    def local(src, dst):
        i = lcount[0]
        lcount[0] += 1
        copy = pltpu.make_async_copy(src, dst, lsem.at[i])
        copy.start()
        return copy

    my_cols = pl.ds(aligned(c * COLS, COLS), COLS)
    sib_cols = pl.ds(aligned((1 - c) * COLS, COLS), COLS)
    my_toks = pl.ds(aligned(c * TOK, TOK), TOK)
    sib_toks = pl.ds(aligned((1 - c) * TOK, TOK), TOK)

    w_load = local(w_ref.at[:, my_cols], W.at[z, p])
    loads = [local(cot_ref.at[:, my_cols], COT.at[my_toks])]
    for q in range(8):
        loads.append(local(tok_ref.at[:, pl.ds(q * PAIR, PAIR)], X.at[q, my_toks]))

    partners = [dev(dx=i) for i in range(1, 4)] + [dev(dy=i) for i in range(1, 4)]
    partners += [dev(dz=i) for i in range(1, 8)] + [dev(dx=i, dy=2) for i in range(1, 4)] + [sibling]
    barrier = pltpu.get_barrier_semaphore()
    for to in partners:
        pl.semaphore_signal(barrier, inc=1, device_id=to, device_id_type=MESH)
    pl.semaphore_wait(barrier, len(partners))

    crow = [pl.ds(k * CH, CH) for k in range(2)]
    arow = [pl.ds(aligned(CR + x * AQ + k * AH, AH), AH) for k in range(2)]
    axq = pl.ds(aligned(CR + x * AQ, AQ), AQ)
    cp, seen = {}, set()

    def at_step(sig, d):
        return 0 if d == 0 else 7 if d == 4 else POS[-sig * d]

    def zc(sig, d, k):
        ref = W.at[zo(at_step(sig, d - 1)), p, crow[k]]
        cp["zc", sig, d, k] = remote("gz", ref, ref, dev(dz=sig % 8))
        send(cp["zc", sig, d, k])

    def za(sig, d):
        rows = axq if d < 4 else arow[0 if sig == 1 else 1]
        ref = W.at[zo(at_step(sig, d - 1)), p, rows]
        cp["za", sig, d] = remote("gz", ref, ref, dev(dz=sig % 8))
        send(cp["za", sig, d])

    def yc(pos, k):
        ref = W.at[zo(pos), p, crow[k]]
        cp["yc", pos, k] = remote("gy", ref, ref, dev(dy=1 if k == 0 else 3))
        send(cp["yc", pos, k])

    def ya(pos, k):
        ref = W.at[zo(pos), p, arow[k]]
        cp["ya", pos, k] = remote("gy", ref, ref, dev(dy=1 if k == 0 else 3))
        send(cp["ya", pos, k])

    def half_of(quarter, k):
        return pl.ds(aligned(CR + (quarter % 4) * AQ + k * AH, AH), AH)

    def xs(pos):
        for k in range(2):
            got("ya", pos, k)
        ref = W.at[zo(pos), pl.ds(1 - p, 1), axq] if pos == 0 else W.at[zo(pos), :, axq]
        for way in range(2):
            cp["xs", pos, way] = remote("gx", ref, ref, dev(dx=1 if way == 0 else 3))
            send(cp["xs", pos, way])

    def xr(pos, way):
        got("xs", pos, way)
        rows = half_of(x + (3 if way == 0 else 1), way)
        ref = W.at[zo(pos), pl.ds(1 - p, 1), rows] if pos == 0 else W.at[zo(pos), :, rows]
        cp["xr", pos, way] = remote("gx", ref, ref, dev(dx=1 if way == 0 else 3))
        send(cp["xr", pos, way])

    def got(*key):
        if key not in seen:
            seen.add(key)
            cp[key].wait_recv()

    def project(pos, first=False):
        at = zo(pos)

        @pl.loop(0, 2)
        def _(i):
            rows = pl.ds(aligned(i * TOK, TOK), TOK)
            part = jnp.dot(X[at, rows], W[at].reshape(PAIR, COLS), preferred_element_type=F32)
            if first:
                ACC[rows] = part
            else:
                ACC[rows] += part

    def positions(d):
        return [0] if d == 0 else [7] if d == 4 else [POS[d], POS[-d]]

    def a_step(d):
        for sig in (1, -1):
            got("za", sig, d)
            if d < 4:
                za(sig, d + 1)
                for k in range(2):
                    ya(at_step(sig, d), k)
            else:
                ya(7, 0 if sig == 1 else 1)

    def ax_step(d):
        for pos in positions(d):
            xs(pos)

    def xr_step(d):
        for pos in positions(d):
            xr(pos, 0)
            xr(pos, 1)

    def c_step(d, j):
        for sig in (1, -1):
            k = j if sig == 1 else 1 - j
            got("zc", sig, d, k)
            if d < 3 or (d == 3 and j == 0):
                zc(sig, d + 1, k)
            yc(at_step(sig, d), k)

    def finish(d):
        for pos in positions(d):
            for k in range(2):
                got("yc", pos, k)
            for way in range(2):
                got("xs", pos, way)
                got("xr", pos, way)
            project(pos, first=pos == 0)

    w_load.wait()
    za(1, 1)
    za(-1, 1)
    ya(0, 0)
    ya(0, 1)
    zc(1, 1, 0)
    zc(-1, 1, 1)
    yc(0, 0)
    yc(0, 1)
    swaps = [remote("swap", cot_ref.at[:, sib_cols], COT.at[my_toks], sibling)]
    for q in range(8):
        swaps.append(remote("swap", tok_ref.at[:, pl.ds(q * PAIR, PAIR)], X.at[q, my_toks], sibling))
    for copy in swaps:
        send(copy)
    a_step(1)
    zc(1, 1, 1)
    zc(-1, 1, 0)
    ax_step(0)
    c_step(1, 0)
    a_step(2)
    ax_step(1)
    c_step(1, 1)
    a_step(3)
    c_step(2, 0)
    ax_step(2)
    xr_step(0)
    a_step(4)
    c_step(2, 1)
    xr_step(1)
    ax_step(3)
    ax_step(4)
    c_step(3, 0)
    xr_step(2)
    for copy in loads:
        copy.wait()
    for copy in swaps:
        copy.wait_recv()
    finish(0)
    c_step(3, 1)
    xr_step(3)
    c_step(4, 0)
    xr_step(4)
    finish(1)
    finish(2)
    finish(3)
    finish(4)

    gain = gain_ref[0:1, my_cols]

    lane = lax.broadcasted_iota(jnp.int32, (128, 128), 1)
    stats = []
    for i in range(4):
        rows = pl.ds(i * 128, 128)
        proj = ACC[rows]
        scaled = COT[rows].astype(F32) * gain
        ssq = jnp.sum(proj * proj, axis=1, keepdims=True)
        sdot = jnp.sum(scaled * proj, axis=1, keepdims=True)
        ST[rows] = jnp.where(lane < 64, ssq, sdot)
        stats.append(remote("stat", ST.at[rows], STR.at[rows], sibling))
        send(stats[i])
    gain_part = jnp.zeros((1, COLS), F32)
    for i in range(4):
        rows = pl.ds(i * 128, 128)
        stats[i].wait_recv()
        both = ST[rows] + STR[rows]
        ssq = both[:, 0:1] * (1.0 / (2 * COLS))
        sdot = both[:, 64:65] * (1.0 / (2 * COLS))
        inverse = lax.rsqrt(ssq + 1e-06)
        normed = ACC[rows] * inverse
        cot = COT[rows].astype(F32)
        scaled = cot * gain
        GK[rows] = (inverse * (scaled - normed * (inverse * sdot))).astype(BF16)
        gain_part += jnp.sum(cot * normed, axis=0, keepdims=True)
    GX[x] = gain_part

    other = 1 - p
    half = [pl.ds(CR + k * AH, AH) for k in range(2)]

    def partial(pos):
        G[zo(pos)] = lax.dot_general(
            X[zo(pos)], GK[...], (((0,), (0,)), ((), ())), preferred_element_type=F32
        ).astype(BF16).reshape(2, ROWS, COLS)

    def y_wide(pos):
        for k in range(2):
            cp["yw", pos, k] = remote("ry", G.at[zo(pos), other, crow[k]], YR.at[pos, crow[k]], dev(dy=1 if k == 0 else 3))
            send(cp["yw", pos, k])

    def x_far(pos):
        for way in range(2):
            rows = half_of(x + 2, way)
            cp["x1", pos, way] = remote("rx", G.at[zo(pos), :, rows], XR.at[pos, way, 0], dev(dx=1 if way == 0 else 3))
            send(cp["x1", pos, way])

    def x_near(pos):
        for way in range(2):
            step = 1 if way == 0 else 3
            rows = half_of(x + step, 1 - way)
            cp["x2", pos, way] = remote("rx", G.at[zo(pos), :, rows], XR.at[pos, way, 1], dev(dx=step))
            send(cp["x2", pos, way])

    def x_second(pos, way):
        at = zo(pos)
        step = 1 if way == 0 else 3
        rows = half_of(x + step, way)
        got("x1", pos, way)
        for parity in range(2):
            G[at, parity, rows] = (G[at, parity, rows].astype(F32) + XR[pos, way, 0, parity].astype(F32)).astype(BF16)
        cp["x3", pos, way] = remote("rx", G.at[at, :, rows], XR.at[pos, way, 2], dev(dx=step))
        send(cp["x3", pos, way])

    def x_third(pos):
        at = zo(pos)
        for way in range(2):
            got("x2", pos, way)
            got("x3", pos, way)
        for k in range(2):
            for parity in range(2):
                total = G[at, parity, arow[k]].astype(F32) + XR[pos, k, 2, parity].astype(F32)
                total = total + XR[pos, 1 - k, 1, parity].astype(F32)
                G[at, parity, arow[k]] = total.astype(BF16)
        for k in range(2):
            cp["yn", pos, k] = remote("ry", G.at[at, other, arow[k]], YR.at[pos, half[k]], dev(dy=1 if k == 0 else 3))
            send(cp["yn", pos, k])

    def owner(sig, d):
        return 0 if d == 0 else 7 if d == 4 else POS[sig * d]

    def first_half(sig):
        return 0 if sig == 1 else 1

    def z_sum(sig, d, k, name):
        pos, at, way = owner(sig, d), zo(owner(sig, d)), 0 if sig == 1 else 1
        rows, buf = (crow[k], crow[k]) if name == "w" else (arow[k], half[k])
        got("y" + name, pos, k)
        total = G[at, p, rows].astype(F32) + YR[pos, buf].astype(F32)
        if d < 3 or (d == 3 and k == first_half(sig)):
            got("z" + name, sig, d, k)
            total = total + ZR[way, d, buf].astype(F32)
        G[at, p, rows] = total.astype(BF16)
        cp["z" + name, sig, d - 1, k] = remote("rz", G.at[at, p, rows], ZR.at[way, d - 1, buf], dev(dz=sig % 8))
        send(cp["z" + name, sig, d - 1, k])

    gtc = {}

    def gt(pos):
        at = zo(pos)
        weight = W[at].reshape(PAIR, COLS)
        TS[pos] = lax.dot_general(
            GK[sib_toks], weight, (((1,), (1,)), ((), ())), preferred_element_type=F32
        ).astype(BF16)
        copy = remote("gt", TS.at[pos], TR.at[pos], sibling)
        gtc[pos] = copy
        send(copy)
        TM[pos] = lax.dot_general(
            GK[my_toks], weight, (((1,), (1,)), ((), ())), preferred_element_type=F32
        )

    def gt_end(pos):
        gtc[pos].wait_recv()
        gt_ref[:, pl.ds(aligned(zo(pos) * PAIR, 128), PAIR)] = (TM[pos] + TR[pos].astype(F32)).astype(BF16)

    def gain_send(name, buf, mine, hops):
        for hop in hops:
            cp["gain" + name, hop] = remote("gg", buf.at[mine], buf.at[mine], dev(**{"d" + name: hop}))
            send(cp["gain" + name, hop])

    def gain_sum(name, buf, hops):
        for hop in hops:
            got("gain" + name, hop)
        total = buf[0]
        for i in range(1, len(hops) + 1):
            total = total + buf[i]
        return total

    def gain_step(i):
        if i == 0:
            gain_send("x", GX, x, (1, 3, 2))
        elif i == 1:
            GY[y] = gain_sum("x", GX, (1, 3, 2))
            gain_send("y", GY, y, (1, 3, 2))
        elif i == 2:
            GZ[z] = gain_sum("y", GY, (1, 3, 2))
            gain_send("z", GZ, z, (1, 7, 2, 6, 3, 5, 4))
        else:
            GB[...] = gain_sum("z", GZ, (1, 7, 2, 6, 3, 5, 4)) * (1.0 / DEVICES)

    gain_step(0)
    partial(7)
    x_far(7)
    y_wide(7)
    partial(5)
    x_near(7)
    partial(6)
    x_far(5)
    partial(3)
    x_near(5)
    y_wide(5)
    partial(4)
    x_second(7, 0)
    x_second(7, 1)
    partial(1)
    partial(2)
    x_far(6)
    partial(0)
    x_near(6)
    z_sum(-1, 4, 1, 'w')
    y_wide(6)
    z_sum(1, 4, 0, 'w')
    x_far(3)
    x_second(5, 1)
    x_second(5, 0)
    gt(7)
    x_third(7)
    gt(5)
    x_near(3)
    y_wide(3)
    z_sum(1, 3, 1, 'w')
    x_second(6, 0)
    x_second(6, 1)
    gt(6)
    x_far(4)
    x_second(3, 0)
    x_second(3, 1)
    gt(3)
    z_sum(-1, 3, 1, 'w')
    gain_step(1)
    z_sum(1, 4, 0, 'n')
    z_sum(-1, 4, 1, 'n')
    y_wide(4)
    x_near(4)
    z_sum(1, 3, 0, 'w')
    z_sum(-1, 3, 0, 'w')
    x_third(5)
    x_far(1)
    x_third(6)
    gt(4)
    x_near(1)
    x_second(4, 0)
    z_sum(1, 2, 1, 'w')
    x_second(4, 1)
    x_third(3)
    gt(1)
    x_far(2)
    y_wide(1)
    gt(2)
    x_near(2)
    x_second(1, 1)
    z_sum(-1, 2, 1, 'w')
    z_sum(1, 2, 0, 'w')
    z_sum(1, 3, 1, 'n')
    z_sum(1, 3, 0, 'n')
    x_second(1, 0)
    z_sum(-1, 3, 1, 'n')
    z_sum(-1, 3, 0, 'n')
    x_third(4)
    x_far(0)
    gain_step(2)
    gt(0)
    x_near(0)
    z_sum(-1, 2, 0, 'w')
    y_wide(2)
    x_second(2, 0)
    x_second(2, 1)
    x_third(1)
    z_sum(1, 1, 1, 'w')
    x_second(0, 0)
    x_second(0, 1)
    y_wide(0)
    z_sum(1, 1, 0, 'w')
    z_sum(-1, 2, 1, 'n')
    z_sum(1, 2, 1, 'n')
    z_sum(-1, 2, 0, 'n')
    z_sum(1, 2, 0, 'n')
    x_third(2)
    z_sum(-1, 1, 1, 'w')
    x_third(0)
    z_sum(-1, 1, 0, 'w')
    z_sum(-1, 1, 0, 'n')
    z_sum(-1, 1, 1, 'n')
    z_sum(1, 1, 1, 'n')
    z_sum(1, 1, 0, 'n')

    others = [(1, 0), (3, 0), (2, 0), (0, 1), (1, 1), (3, 1), (2, 1)]

    def wide_block(dx, dh):
        return pl.ds(aligned((h + dh) % 2 * CH, CH), CH), pl.ds(aligned((x + dx + 4) % 4 * 128, 128), 128)

    def narrow_block(dx, dh):
        return pl.ds(aligned(CR + (x + dx + 4) % 4 * AQ + (h + dh) % 2 * AH, AH), AH)

    for sig in (1, -1):
        for k in range(2):
            got("zw", sig, 0, k)
    for k in range(2):
        got("yw", 0, k)
    mine = YR[0, 0:CR].astype(F32) + G[z, p, 0:CR].astype(F32)
    mine = mine + ZR[0, 0, 0:CR].astype(F32) + ZR[1, 0, 0:CR].astype(F32)
    SF[...] = mine
    SB[...] = mine.astype(BF16)
    for i, (dx, dh) in enumerate(others):
        cp["ax", i] = remote("ax", SB.at[wide_block(dx, dh)], AX.at[i], dev(dx=dx, dy=2 * dh))
        send(cp["ax", i])
    for sig in (1, -1):
        for k in range(2):
            got("zn", sig, 0, k)
    for k in range(2):
        got("yn", 0, k)
    last = G[z, p, axq].astype(F32) + YR[0, CR:].astype(F32)
    NB[...] = last + ZR[0, 0, CR:].astype(F32) + ZR[1, 0, CR:].astype(F32)
    ah = remote("ah", NB.at[pl.ds(aligned((1 - h) * AH, AH), AH)], NR, dev(dy=2))
    send(ah)
    for q in (7, 5, 6, 3, 4, 1, 2, 0):
        gt_end(q)
    def hand_out(name, ref):
        for i, (dx, dh) in enumerate(others):
            cp[name, i] = remote("af", ref, ref, dev(dx=dx, dy=2 * dh))
            send(cp[name, i])
        far.append(remote("ac", ref, ref, sibling))
        send(far[-1])

    far = []
    ah.wait_recv()
    FO[c, narrow_block(0, 0)] = ((NB[pl.ds(aligned(h * AH, AH), AH)] + NR[...]) * (1.0 / DEVICES)).astype(BF16)
    hand_out("narrow", FO.at[c, narrow_block(0, 0)])
    total = SF[wide_block(0, 0)]
    for i in range(len(others)):
        got("ax", i)
        total = total + AX[i].astype(F32)
    FO[(c,) + wide_block(0, 0)] = (total * (1.0 / DEVICES)).astype(BF16)
    hand_out("wide", FO.at[(c,) + wide_block(0, 0)])
    gain_step(3)
    gg_out = [local(GB, gg_ref.at[:, my_cols])]
    gg_far = remote("go", GB, gg_ref.at[:, my_cols], sibling)
    send(gg_far)

    for i, (dx, dh) in enumerate(others):
        for name, ref in (("narrow", FO.at[c, narrow_block(-dx, dh)]), ("wide", FO.at[(c,) + wide_block(-dx, dh)])):
            got(name, i)
            far.append(remote("ac", ref, ref, sibling))
            send(far[-1])
    for copy in far:
        copy.wait_recv()
    gw_ref[...] = FO[...]
    gg_far.wait_recv()
    for copy in gg_out:
        copy.wait()
    for copy in open_sends:
        copy.wait_send()


def finish(gt_in, gw_in, gg_in, gt_ref, gw_ref, gg_ref, wide, sem):
    copies = []
    for i in range(4):
        rows = pl.ds(i * TOK // 4, TOK // 4)
        copies.append(pltpu.make_async_copy(gt_in.at[rows], gt_ref.at[rows], sem.at[i]))
    copies.append(pltpu.make_async_copy(gg_in, gg_ref, sem.at[4]))
    for copy in copies:
        copy.start()
    for i in range(2):
        rows = pl.ds(i * ROWS // 2, ROWS // 2)
        for half in range(2):
            wide[rows, half * COLS : (half + 1) * COLS] = gw_in[half, rows].astype(F32)
        copies.append(pltpu.make_async_copy(wide.at[rows], gw_ref.at[rows], sem.at[5 + i]))
        copies[-1].start()
    for copy in copies:
        copy.wait()


SEMS = {"gz": 30, "gy": 32, "gx": 32, "swap": 9, "stat": 4, "rx": 48, "ry": 32, "rz": 28, "gt": 8, "gg": 13,
        "go": 1, "ax": 7, "ah": 1, "af": 14, "ac": 16}
GROUPS = tuple(SEMS)


def per_device(tokens, key_weight, key_gain, key_cotangent):
    anywhere = pl.BlockSpec(memory_space=pl.ANY)
    vmem = pl.BlockSpec(memory_space=pltpu.VMEM)
    sems = []
    for group in GROUPS:
        sems += [pltpu.SemaphoreType.DMA((SEMS[group],))] * 2
    V = pltpu.VMEM
    grad_tokens, grad_weight, grad_gain = pl.pallas_call(
        kernel,
        out_shape=(
            pltpu.VMEM((TOK, 5120), BF16),
            pltpu.VMEM((2, ROWS, COLS), BF16),
            pltpu.VMEM((1, 1024), F32),
        ),
        in_specs=[anywhere, anywhere, vmem, anywhere],
        out_specs=(vmem, vmem, vmem),
        scratch_shapes=[
            V((8, 2, ROWS, COLS), BF16),
            V((8, 2 * TOK, PAIR), BF16),
            V((2 * TOK, COLS), BF16),
            V((2 * TOK, COLS), F32),
            V((2 * TOK, COLS), BF16),
            V((2 * TOK, 128), F32),
            V((2 * TOK, 128), F32),
            V((8, 2, ROWS, COLS), BF16),
            V((8, 2, 3, 2, AH, COLS), BF16),
            V((8, CR + AQ, COLS), BF16),
            V((2, 4, CR + AQ, COLS), BF16),
            V((CR, COLS), BF16),
            V((CR, COLS), F32),
            V((7, CH, 128), BF16),
            V((AQ, COLS), F32),
            V((AH, COLS), F32),
            V((2, ROWS, COLS), BF16),
            V((8, TOK, PAIR), BF16),
            V((8, TOK, PAIR), BF16),
            V((8, TOK, PAIR), F32),
            V((1, COLS), F32),
            V((4, 1, COLS), F32),
            V((4, 1, COLS), F32),
            V((8, 1, COLS), F32),
            pltpu.SemaphoreType.DMA((24,)),
            *sems,
        ],
        compiler_params=pltpu.CompilerParams(
            collective_id=0, has_side_effects=True, vmem_limit_bytes=58 * 2**20
        ),
        name="key_projection_backward",
    )(tokens, key_weight, key_gain.reshape(1, 1024), key_cotangent)
    grad_tokens, grad_weight, grad_gain = pl.pallas_call(
        finish,
        out_shape=(
            jax.ShapeDtypeStruct((TOK, 5120), BF16),
            jax.ShapeDtypeStruct((ROWS, 1024), F32),
            jax.ShapeDtypeStruct((1, 1024), F32),
        ),
        in_specs=[vmem, vmem, vmem],
        out_specs=(anywhere, anywhere, anywhere),
        scratch_shapes=[pltpu.VMEM((ROWS, 1024), F32), pltpu.SemaphoreType.DMA((7,))],
        compiler_params=pltpu.CompilerParams(vmem_limit_bytes=16 * 2**20),
        name="write_results",
    )(grad_tokens, grad_weight, grad_gain)
    return grad_tokens, grad_weight, grad_gain.reshape(1024)


def solution(mesh):
    return jax.shard_map(
        per_device,
        mesh=mesh,
        in_specs=(P(("rep", "shard"), None), P("shard", None), P(), P(("rep", "shard"), None)),
        out_specs=(P(("rep", "shard"), None), P("shard", None), P()),
        check_vma=False,
    )
```

time: 103 us -> 92 us (0.89)
  Pallas kernels: 102 us -> 91.1 us
    pallas_call x1, Pallas kernels: 97.1 us -> 89.1 us  [per_device(): pl.pallas_call(kernel, out_shape=(pltpu.VMEM((TOK, 5120), BF16), pltpu.VM...]
    pallas_call x1, Pallas kernels: 4.79 us -> 1.98 us  [per_device(): pl.pallas_call(finish, out_shape=(jax.ShapeDtypeStruct((TOK, 5120), BF16)...]
where the time goes in v3:
time: 92 us; the launch traced here: 91.9 us
  Pallas kernels  91.1 us (99%)
    pallas_call x1, Pallas kernels, per_device(): pl.pallas_call(kernel, out_shape=(pltpu.VMEM((TOK, 5120), BF16), pltpu.VM...  89.1 us
    pallas_call x1, Pallas kernels, per_device(): pl.pallas_call(finish, out_shape=(jax.ShapeDtypeStruct((TOK, 5120), BF16)...  1.98 us

profile of v3, /device:TPU:1, one launch (start us, length us, event | category | flops | bytes accessed | tf_op | source)
XLA Modules:
  0.0 91.9 jit_solution(2724541319470672119)
XLA Ops:
  0.6 89.1 %key_projection_backward.1 = (bf16[256,5120]{1,0:T(8,128)(2,1)S(1)}, bf16[2,320,512]{2,1,0:T(8,128)(2,1)S(1)}, f32[1,1024]{1,0:T(1,128)S(1)}) custom-call(bf16[256,5120]{1,0:T(8,128)(2,1)} %tok_ref.1, bf16[320,1024]{1,0:T(8,128)(2,1)} %w_ref.1, f32[1,1024]{1,0:T(1,128)} %bitcast.2, bf16[256,1024]{1,0:T(8,128)(2,1)} %cot_ref.1), custom_call_target="tpu_custom_call" | custom-call | tf_op jit(solution)/shard_map/key_projection_backward/pallas_call | solution.py:578
  89.7 2.0 %write_results.1 = (bf16[256,5120]{1,0:T(8,128)(2,1)}, f32[320,1024]{1,0:T(8,128)}, f32[1,1024]{1,0:T(1,128)}) custom-call(bf16[256,5120]{1,0:T(8,128)(2,1)S(1)} %get-tuple-element.9.gt_in, bf16[2,320,512]{2,1,0:T(8,128)(2,1)S(1)} %get-tuple-element.10.gw_in, f32[1,1024]{1,0:T(1,128)S(1)} %get-tuple-element.11.gg_in), custom_call_target="tpu_custom_call" | custom-call | tf_op jit(solution)/shard_map/write_results/pallas_call | solution.py:620

commit v4 on v3

--- a/solution.py
+++ b/solution.py
@@ -430,16 +430,13 @@
     x_third(5)
     x_far(1)
     x_third(6)
-    gt(4)
     x_near(1)
     x_second(4, 0)
     z_sum(1, 2, 1, 'w')
     x_second(4, 1)
     x_third(3)
-    gt(1)
     x_far(2)
     y_wide(1)
-    gt(2)
     x_near(2)
     x_second(1, 1)
     z_sum(-1, 2, 1, 'w')
@@ -452,7 +449,6 @@
     x_third(4)
     x_far(0)
     gain_step(2)
-    gt(0)
     x_near(0)
     z_sum(-1, 2, 0, 'w')
     y_wide(2)
@@ -506,7 +502,9 @@
     NB[...] = last + ZR[0, 0, CR:].astype(F32) + ZR[1, 0, CR:].astype(F32)
     ah = remote("ah", NB.at[pl.ds(aligned((1 - h) * AH, AH), AH)], NR, dev(dy=2))
     send(ah)
-    for q in (7, 5, 6, 3, 4, 1, 2, 0):
+    for q in (4, 1, 2, 0):
+        gt(q)
+    for q in (7, 5, 6, 3):
         gt_end(q)
     def hand_out(name, ref):
         for i, (dx, dh) in enumerate(others):
@@ -530,6 +528,8 @@
     gg_far = remote("go", GB, gg_ref.at[:, my_cols], sibling)
     send(gg_far)
 
+    for q in (4, 1, 2, 0):
+        gt_end(q)
     for i, (dx, dh) in enumerate(others):
         for name, ref in (("narrow", FO.at[c, narrow_block(-dx, dh)]), ("wide", FO.at[(c,) + wide_block(-dx, dh)])):
             got(name, i)

time: 92 us -> 91.5 us (level)
  no operation moved by 1% of the time
where the time goes in v4:
time: 91.5 us; the launch traced here: 91.3 us
  Pallas kernels  90.5 us (99%)
    pallas_call x1, Pallas kernels, per_device(): pl.pallas_call(kernel, out_shape=(pltpu.VMEM((TOK, 5120), BF16), pltpu.VM...  88.6 us
    pallas_call x1, Pallas kernels, per_device(): pl.pallas_call(finish, out_shape=(jax.ShapeDtypeStruct((TOK, 5120), BF16)...  1.98 us

profile of v4, /device:TPU:1, one launch (start us, length us, event | category | flops | bytes accessed | tf_op | source)
XLA Modules:
  0.0 91.3 jit_solution(9651386265652107143)
XLA Ops:
  0.6 88.6 %key_projection_backward.1 = (bf16[256,5120]{1,0:T(8,128)(2,1)S(1)}, bf16[2,320,512]{2,1,0:T(8,128)(2,1)S(1)}, f32[1,1024]{1,0:T(1,128)S(1)}) custom-call(bf16[256,5120]{1,0:T(8,128)(2,1)} %tok_ref.1, bf16[320,1024]{1,0:T(8,128)(2,1)} %w_ref.1, f32[1,1024]{1,0:T(1,128)} %bitcast.2, bf16[256,1024]{1,0:T(8,128)(2,1)} %cot_ref.1), custom_call_target="tpu_custom_call" | custom-call | tf_op jit(solution)/shard_map/key_projection_backward/pallas_call | solution.py:578
  89.2 2.0 %write_results.1 = (bf16[256,5120]{1,0:T(8,128)(2,1)}, f32[320,1024]{1,0:T(8,128)}, f32[1,1024]{1,0:T(1,128)}) custom-call(bf16[256,5120]{1,0:T(8,128)(2,1)S(1)} %get-tuple-element.9.gt_in, bf16[2,320,512]{2,1,0:T(8,128)(2,1)S(1)} %get-tuple-element.10.gw_in, f32[1,1024]{1,0:T(1,128)S(1)} %get-tuple-element.11.gg_in), custom_call_target="tpu_custom_call" | custom-call | tf_op jit(solution)/shard_map/write_results/pallas_call | solution.py:620

commit v5 on v4

--- a/solution.py
+++ b/solution.py
@@ -220,8 +220,8 @@
     c_step(2, 0)
     ax_step(2)
     xr_step(0)
+    c_step(2, 1)
     a_step(4)
-    c_step(2, 1)
     xr_step(1)
     ax_step(3)
     ax_step(4)

time: 91.5 us -> 92 us (level)
  no operation moved by 1% of the time
where the time goes in v5:
time: 92 us; the launch traced here: 91.9 us
  Pallas kernels  91.1 us (99%)
    pallas_call x1, Pallas kernels, per_device(): pl.pallas_call(kernel, out_shape=(pltpu.VMEM((TOK, 5120), BF16), pltpu.VM...  89.1 us
    pallas_call x1, Pallas kernels, per_device(): pl.pallas_call(finish, out_shape=(jax.ShapeDtypeStruct((TOK, 5120), BF16)...  1.98 us

profile of v5, /device:TPU:1, one launch (start us, length us, event | category | flops | bytes accessed | tf_op | source)
XLA Modules:
  0.0 91.9 jit_solution(622843107945746633)
XLA Ops:
  0.6 89.1 %key_projection_backward.1 = (bf16[256,5120]{1,0:T(8,128)(2,1)S(1)}, bf16[2,320,512]{2,1,0:T(8,128)(2,1)S(1)}, f32[1,1024]{1,0:T(1,128)S(1)}) custom-call(bf16[256,5120]{1,0:T(8,128)(2,1)} %tok_ref.1, bf16[320,1024]{1,0:T(8,128)(2,1)} %w_ref.1, f32[1,1024]{1,0:T(1,128)} %bitcast.2, bf16[256,1024]{1,0:T(8,128)(2,1)} %cot_ref.1), custom_call_target="tpu_custom_call" | custom-call | tf_op jit(solution)/shard_map/key_projection_backward/pallas_call | solution.py:578
  89.7 2.0 %write_results.1 = (bf16[256,5120]{1,0:T(8,128)(2,1)}, f32[320,1024]{1,0:T(8,128)}, f32[1,1024]{1,0:T(1,128)}) custom-call(bf16[256,5120]{1,0:T(8,128)(2,1)S(1)} %get-tuple-element.9.gt_in, bf16[2,320,512]{2,1,0:T(8,128)(2,1)S(1)} %get-tuple-element.10.gw_in, f32[1,1024]{1,0:T(1,128)S(1)} %get-tuple-element.11.gg_in), custom_call_target="tpu_custom_call" | custom-call | tf_op jit(solution)/shard_map/write_results/pallas_call | solution.py:620
